TPU v7x, 128 devices: a whole 4x4x4 slice. The times are simulated.
128 devices in a mesh: pipe: 4 (over z_hi, core), expert: 32 (over y, z_lo, x).
Axes of the slice: x: 4, y: 4, z: 4 (z_hi: 2, z_lo: 2; z = z_hi * 2 + z_lo), core: 2. Of those that a mesh axis runs over, the one named last changes fastest.
Arguments:
- fwd_src: bfloat16 [4, 2048, 7168], P('pipe', 'expert'), may hold values from -12.65 to 12.65
- fwd_route: int32 [4, 2048, 1], P('pipe', 'expert'), may hold values from 0 to 7, as said below
- bwd_input: bfloat16 [4, 2048, 7168], P('pipe', 'expert'), may hold values from -12.65 to 12.65
- bwd_expert_out: bfloat16 [4, 2048, 7168], P('pipe', 'expert'), may hold values from -4 to 4
- grad_src: bfloat16 [4, 2048, 7168], P('pipe', 'expert'), may hold values from -5 to 5
- bwd_route: int32 [4, 2048, 1], P('pipe', 'expert'), may hold values from 0 to 7, as said below
- norm_gain: bfloat16 [4, 7168], P('pipe'), may hold values from 0.099609375 to 1.8984375
- router: bfloat16 [4, 7168, 8], P('pipe'), may hold values from -0.0625 to 0.0625
- gate_w: bfloat16 [4, 7168, 8192], P('pipe', None, 'expert'), may hold values from -0.0625 to 0.0625
- up_w: bfloat16 [4, 7168, 8192], P('pipe', None, 'expert'), may hold values from -0.0625 to 0.0625
- down_w: bfloat16 [4, 8192, 7168], P('pipe', 'expert'), may hold values from -0.1875 to 0.1875
Outputs:
- fwd_out: bfloat16 [4, 2048, 7168], P('pipe', 'expert')
- bwd_out: bfloat16 [4, 2048, 7168], P('pipe', 'expert')
Inputs may be any that keep to these rules, and one draw needn't show every extreme that they name: `fwd_route`: at every section one expert, drawn from the seed, is chosen by exactly 16 of the 64 tokens of every device; no expert is chosen by more than 16 of the tokens of one device. `bwd_route`: at every section one expert, drawn from the seed, is chosen by exactly 16 of the 64 tokens of every device; no expert is chosen by more than 16 of the tokens of one device.
All inputs are finite; a program needn't handle non-finite values.
Results may differ from a plain program's by a relative error of at most 0.009.
Values may be sent and summed in bfloat16 or wider, within the bound.
A program may use at most 192 MiB of HBM per device.

v0:
```python
import jax
import jax.numpy as jnp
from jax import lax
from jax.sharding import PartitionSpec as P

EXPERTS = 8
MOST = 16


norm_eps = 1e-06
route_scale = 2.5


def passed_along(block, axis, distance):
    devices = range(lax.axis_size(axis))
    route = [((i - distance) % len(devices), i) for i in devices]
    return lax.ppermute(block, axis, route)


def rms_norm(values, gain_row):
    widened = values.astype(jnp.float32)
    inv_scale = lax.rsqrt(jnp.mean(widened * widened, axis=-1, keepdims=True) + norm_eps)
    normed = (widened * inv_scale * gain_row.astype(jnp.float32)).astype(jnp.bfloat16)
    return (normed, inv_scale)


def slot_layout(chosen):
    token_count = chosen.shape[0]
    one_hot = (chosen[:, None] == jnp.arange(EXPERTS, dtype=jnp.int32)[None, :]).astype(jnp.float32)
    earlier = (jnp.arange(token_count)[:, None] > jnp.arange(token_count)[None, :]).astype(
        jnp.float32
    )
    prior_counts = jnp.dot(earlier, one_hot, precision=lax.Precision.HIGHEST)
    slot_rank = jnp.sum(prior_counts * one_hot, axis=1).astype(jnp.int32)
    slot_index = chosen * MOST + slot_rank
    placing = (jnp.arange(EXPERTS * MOST, dtype=jnp.int32)[:, None] == slot_index[None, :]).astype(
        jnp.bfloat16
    )
    return (one_hot, slot_index, placing)


def route_weight(normed, router_local, one_hot):
    logits = jnp.dot(normed, router_local, preferred_element_type=jnp.float32)
    return jax.nn.sigmoid(jnp.sum(logits * one_hot, axis=1))


def send_back(partial_rows):
    return lax.all_to_all(partial_rows, "expert", split_axis=0, concat_axis=0, tiled=True)


def dispatch(bundle, compute):
    shard_count = lax.axis_size("expert") // EXPERTS
    copied = jnp.broadcast_to(bundle[:, None], (bundle.shape[0], shard_count) + bundle.shape[1:])
    copied = copied.reshape((bundle.shape[0] * shard_count,) + bundle.shape[1:])
    return send_back(
        compute(lax.all_to_all(copied, "expert", split_axis=0, concat_axis=0, tiled=True))
    )


def gather_back(returned, slot_index):
    source_count, slot_count, feature_count = returned.shape
    summed = jnp.sum(
        returned.reshape(EXPERTS, source_count // EXPERTS, slot_count, feature_count).astype(
            jnp.float32
        ),
        axis=1,
    )
    flat_rows = summed.reshape(EXPERTS * slot_count, feature_count)
    return jnp.take(flat_rows, slot_index, axis=0)


def shards(
    fwd_src,
    fwd_route,
    bwd_input,
    bwd_expert_out,
    grad_src,
    bwd_route,
    norm_gain,
    router,
    gate_w,
    up_w,
    down_w,
):
    arriving = passed_along(fwd_src, "pipe", 1)[0]
    incoming = passed_along(grad_src, "pipe", -1)[0]
    gain_row = norm_gain[0]
    router_local = router[0]
    w_gate = gate_w[0]
    w_up = up_w[0]
    w_down = down_w[0]
    feature_count = arriving.shape[1]

    def forward_compute(received):
        source_count, slot_count, width_in = received.shape
        flat_rows = received.reshape(source_count * slot_count, width_in)
        gate_pre = jnp.dot(flat_rows, w_gate, preferred_element_type=jnp.float32)
        up_pre = jnp.dot(flat_rows, w_up, preferred_element_type=jnp.float32)
        hidden = (jax.nn.silu(gate_pre) * up_pre).astype(jnp.bfloat16)
        partial_out = jnp.dot(hidden, w_down, preferred_element_type=jnp.float32).astype(
            jnp.bfloat16
        )
        return partial_out.reshape(source_count, slot_count, width_in)

    def backward_compute(received):
        source_count, slot_count, doubled = received.shape
        width_in = doubled // 2
        flat_rows = received.reshape(source_count * slot_count, doubled)
        rows_in = flat_rows[:, :width_in]
        grads_in = flat_rows[:, width_in:]
        gate_pre = jnp.dot(rows_in, w_gate, preferred_element_type=jnp.float32)
        up_pre = jnp.dot(rows_in, w_up, preferred_element_type=jnp.float32)
        gate_sigmoid = jax.nn.sigmoid(gate_pre)
        back_hidden = lax.dot_general(
            grads_in, w_down, (((1,), (1,)), ((), ())), preferred_element_type=jnp.float32
        )
        d_gate = (
            back_hidden * up_pre * gate_sigmoid * (1.0 + gate_pre * (1.0 - gate_sigmoid))
        ).astype(jnp.bfloat16)
        d_up = (back_hidden * gate_pre * gate_sigmoid).astype(jnp.bfloat16)
        partial_in = lax.dot_general(
            d_gate, w_gate, (((1,), (1,)), ((), ())), preferred_element_type=jnp.float32
        )
        partial_in = partial_in + lax.dot_general(
            d_up, w_up, (((1,), (1,)), ((), ())), preferred_element_type=jnp.float32
        )
        partial_in = partial_in.astype(jnp.bfloat16)
        return partial_in.reshape(source_count, slot_count, width_in)

    normed_fwd, scale_fwd = rms_norm(arriving, gain_row)
    hot_fwd, slots_fwd, placing_fwd = slot_layout(fwd_route[0, :, 0])
    weight_fwd = route_weight(normed_fwd, router_local, hot_fwd)
    bundle_fwd = jnp.dot(placing_fwd, normed_fwd, preferred_element_type=jnp.float32).astype(
        jnp.bfloat16
    )
    bundle_fwd = bundle_fwd.reshape(EXPERTS, MOST, feature_count)
    expert_sum = gather_back(dispatch(bundle_fwd, forward_compute), slots_fwd)
    fwd_out = (
        arriving.astype(jnp.float32) + route_scale * weight_fwd[:, None] * expert_sum
    ).astype(jnp.bfloat16)
    normed_bwd, scale_bwd = rms_norm(bwd_input[0], gain_row)
    hot_bwd, slots_bwd, placing_bwd = slot_layout(bwd_route[0, :, 0])
    weight_bwd = route_weight(normed_bwd, router_local, hot_bwd)
    joined = jnp.concatenate([normed_bwd, incoming], axis=1)
    bundle_bwd = jnp.dot(placing_bwd, joined, preferred_element_type=jnp.float32).astype(
        jnp.bfloat16
    )
    bundle_bwd = bundle_bwd.reshape(EXPERTS, MOST, 2 * feature_count)
    input_sum = gather_back(dispatch(bundle_bwd, backward_compute), slots_bwd)
    agreement = jnp.sum(
        incoming.astype(jnp.float32) * bwd_expert_out[0].astype(jnp.float32), axis=1
    )
    d_logit = route_scale * agreement * weight_bwd * (1.0 - weight_bwd)
    router_column = lax.dot_general(
        hot_bwd.astype(jnp.bfloat16),
        router_local,
        (((1,), (1,)), ((), ())),
        preferred_element_type=jnp.float32,
    )
    d_normed = route_scale * weight_bwd[:, None] * input_sum + d_logit[:, None] * router_column
    widened = bwd_input[0].astype(jnp.float32)
    scaled_grad = d_normed * gain_row.astype(jnp.float32)
    d_input = scale_bwd * scaled_grad - widened * scale_bwd**3 * jnp.mean(
        widened * scaled_grad, axis=1, keepdims=True
    )
    bwd_out = (incoming.astype(jnp.float32) + d_input).astype(jnp.bfloat16)
    return (fwd_out[None], bwd_out[None])


def solution(mesh):
    placed = (
        P("pipe", "expert", None),
        P("pipe", "expert", None),
        P("pipe", "expert", None),
        P("pipe", "expert", None),
        P("pipe", "expert", None),
        P("pipe", "expert", None),
        P("pipe", None),
        P("pipe", None, None),
        P("pipe", None, "expert"),
        P("pipe", None, "expert"),
        P("pipe", "expert", None),
    )
    return jax.shard_map(
        shards,
        mesh=mesh,
        in_specs=placed,
        out_specs=(P("pipe", "expert", None), P("pipe", "expert", None)),
        check_vma=False,
    )
```

profile of v0, /device:TPU:8, one launch (start us, length us, event | category | flops | bytes accessed | tf_op | source)
XLA Modules:
  0.0 601.0 jit_solution(11769329972113876442)
XLA Ops:
  0.6 0.0 copy-start
  0.6 0.1 collective-permute-start
  0.7 0.8 mul.256
  1.5 0.9 fusion.73
  2.4 0.7 compare_and_fusion.1
  3.1 12.3 %collective-permute-done = bf16[1,64,7168]{2,1,0:T(8,128)(2,1)S(1)} collective-permute-done((bf16[1,64,7168]{2,1,0:T(8,128)(2,1)}, bf16[1,64,7168]{2,1,0:T(8,128)(2,1)S(1)}, u32[]{:S(2)}, u32[]{:S(2)}) %collective-permute-start) | collective-permute-done | bytes 917536 | tf_op jit(solution)/shard_map/ppermute | solution.py:17
  15.3 0.3 fusion.28
  15.6 0.7 convolution_convert_fusion.2
  16.3 3.9 broadcast_in_dim.22
  20.2 0.0 copy-start.1
  20.2 0.0 copy-start.4
  20.2 9.0 %all-to-all-start = ((bf16[32,16,7168]{2,1,0:T(8,128)(2,1)}), bf16[32,16,7168]{2,1,0:T(8,128)(2,1)}, u32[]{:S(2)}, u32[]{:S(2)}) async-start(bf16[32,16,7168]{2,1,0:T(8,128)(2,1)} %bitcast.134), calls=%async_computation | async-start | bytes 14680064 | tf_op jit(solution)/shard_map/all_to_all | solution.py:56
  29.2 0.1 collective-permute-start.1
  29.3 0.0 copy-done.1
  29.3 0.3 fusion.34
  29.6 0.3 fusion.36
  29.9 0.0 copy-done.4
  29.9 0.1 fusion.74
  30.0 73.8 %collective-permute-done.1 = bf16[1,64,7168]{2,1,0:T(8,128)(2,1)S(1)} collective-permute-done((bf16[1,64,7168]{2,1,0:T(8,128)(2,1)}, bf16[1,64,7168]{2,1,0:T(8,128)(2,1)S(1)}, u32[]{:S(2)}, u32[]{:S(2)}) %collective-permute-start.1) | collective-permute-done | bytes 917536 | tf_op jit(solution)/shard_map/ppermute | solution.py:17
  103.9 3.0 convolution_convert_fusion
  106.9 14.4 %all-to-all-done = bf16[32,16,7168]{2,1,0:T(8,128)(2,1)} async-done(((bf16[32,16,7168]{2,1,0:T(8,128)(2,1)}), bf16[32,16,7168]{2,1,0:T(8,128)(2,1)}, u32[]{:S(2)}, u32[]{:S(2)}) %all-to-all-start) | async-done | bytes 7340064 | tf_op jit(solution)/shard_map/all_to_all | solution.py:56
  121.2 6.6 %broadcast_in_dim.25 = bf16[8,4,16,14336]{3,2,1,0:T(8,128)(2,1)} broadcast(bf16[8,16,14336]{2,1,0:T(8,128)(2,1)} %bitcast.136), dimensions={0,2,3} | broadcast | bytes 18350080 | tf_op jit(solution)/shard_map/broadcast_in_dim | solution.py:53
  127.9 15.1 %all-to-all-start.2 = ((bf16[32,16,14336]{2,1,0:T(8,128)(2,1)}), bf16[32,16,14336]{2,1,0:T(8,128)(2,1)}, u32[]{:S(2)}, u32[]{:S(2)}) async-start(bf16[32,16,14336]{2,1,0:T(8,128)(2,1)} %bitcast.132), calls=%async_computation.2 | async-start | bytes 29360128 | tf_op jit(solution)/shard_map/all_to_all | solution.py:56
  143.0 6.2 %fusion.17 = f32[512,256]{1,0:T(8,128)S(1)} fusion(bf16[512,7168]{1,0:T(8,128)(2,1)} %bitcast.7, bf16[1,7168,256]{2,1,0:T(8,128)(2,1)} %param.21), kind=kOutput, calls=%fused_computation.26 | convolution fusion | flops 1879048192 | bytes 11534336 | tf_op jit(solution)/shard_map/dot_general | solution.py:97
  149.2 16.0 %convolution_convert_fusion.1 = bf16[512,7168]{1,0:T(8,128)(2,1)} fusion(bf16[1,256,7168]{2,1,0:T(8,128)(2,1)} %param.23, bf16[512,7168]{1,0:T(8,128)(2,1)} %bitcast.7, bf16[1,7168,256]{2,1,0:T(8,128)(2,1)} %param.22, f32[512,256]{1,0:T(8,128)S(1)} %fusion.17), kind=kOutput, calls=%fused_computation.6 | convolution fusion | flops 3762552832 | bytes 22544384 | tf_op jit(solution)/shard_map/dot_general | solution.py:100
  165.2 191.6 %all-to-all-done.2 = bf16[32,16,14336]{2,1,0:T(8,128)(2,1)} async-done(((bf16[32,16,14336]{2,1,0:T(8,128)(2,1)}), bf16[32,16,14336]{2,1,0:T(8,128)(2,1)}, u32[]{:S(2)}, u32[]{:S(2)}) %all-to-all-start.2) | async-done | bytes 14680096 | tf_op jit(solution)/shard_map/all_to_all | solution.py:56
  356.8 37.8 %all-to-all-start.1 = ((bf16[32,16,7168]{2,1,0:T(8,128)(2,1)}), bf16[32,16,7168]{2,1,0:T(8,128)(2,1)}, u32[]{:S(2)}, u32[]{:S(2)}) async-start(bf16[32,16,7168]{2,1,0:T(8,128)(2,1)} %bitcast.135), calls=%async_computation.1 | async-start | bytes 14680064 | tf_op jit(solution)/shard_map/all_to_all | solution.py:48
  394.6 0.0 copy-start.2
  394.6 6.4 %fusion.2 = f32[512,256]{1,0:T(8,128)S(1)} fusion(bf16[512,14336]{1,0:T(8,128)(2,1)} %bitcast.21, bf16[1,256,7168]{2,1,0:T(8,128)(2,1)} %param.23), kind=kOutput, calls=%fused_computation.11 | convolution fusion | flops 1879048192 | bytes 11534336 | tf_op jit(solution)/shard_map/dot_general | solution.py:114
  401.0 0.0 copy-done.2
  401.0 6.0 fusion.4
  407.0 18.3 %fusion.14 = f32[512,7168]{1,0:T(8,128)} fusion(bf16[1,7168,256]{2,1,0:T(8,128)(2,1)} %param.21, f32[512,256]{1,0:T(8,128)S(1)} %fusion.2, bf16[1,7168,256]{2,1,0:T(8,128)(2,1)} %param.22, bf16[512,14336]{1,0:T(8,128)(2,1)} %bitcast.21, f32[512,256]{1,0:T(8,128)} %fusion.4), kind=kOutput, calls=%fused_computation.23 | convolution fusion | flops 3759407104 | bytes 30408704 | tf_op jit(solution)/shard_map/dot_general | solution.py:121
  425.3 11.5 %add_convert_fusion = bf16[512,7168]{1,0:T(8,128)(2,1)} fusion(f32[512,7168]{1,0:T(8,128)} %fusion.14, bf16[1,7168,256]{2,1,0:T(8,128)(2,1)} %param.22, f32[512,256]{1,0:T(8,128)S(1)} %fusion.2, f32[512,256]{1,0:T(8,128)} %fusion.4), kind=kOutput, calls=%fused_computation.5 | convolution fusion | flops 1887174656 | bytes 26738688 | tf_op jit(solution)/shard_map/dot_general | solution.py:124
  436.9 48.3 %all-to-all-done.1 = bf16[32,16,7168]{2,1,0:T(8,128)(2,1)} async-done(((bf16[32,16,7168]{2,1,0:T(8,128)(2,1)}), bf16[32,16,7168]{2,1,0:T(8,128)(2,1)}, u32[]{:S(2)}, u32[]{:S(2)}) %all-to-all-start.1) | async-done | bytes 7340064 | tf_op jit(solution)/shard_map/all_to_all | solution.py:48
  485.2 0.0 copy-start.5
  485.2 12.0 %all-to-all-start.3 = ((bf16[32,16,7168]{2,1,0:T(8,128)(2,1)}), bf16[32,16,7168]{2,1,0:T(8,128)(2,1)}, u32[]{:S(2)}, u32[]{:S(2)}) async-start(bf16[32,16,7168]{2,1,0:T(8,128)(2,1)} %bitcast.133), calls=%async_computation.3 | async-start | bytes 14680064 | tf_op jit(solution)/shard_map/all_to_all | solution.py:48
  497.2 0.0 copy-start.3
  497.2 0.0 copy-done
  497.3 0.4 fusion.72
  497.7 0.0 copy-done.5
  497.7 0.4 fusion.71
  498.1 0.2 copy-done.3
  498.4 0.3 fusion.26
  498.7 6.7 %convert_reduce_fusion.1 = f32[8,16,7168]{2,1,0:T(8,128)} fusion(bf16[32,16,7168]{2,1,0:T(8,128)(2,1)} %all-to-all-done.1), kind=kLoop, calls=%fused_computation.4 | loop fusion | flops 6422528 | bytes 11010048 | tf_op jit(solution)/shard_map/reduce_sum | solution.py:62
  505.5 5.1 gather_fusion
  510.6 2.8 fusion.83
  513.4 71.9 %all-to-all-done.3 = bf16[32,16,7168]{2,1,0:T(8,128)(2,1)} async-done(((bf16[32,16,7168]{2,1,0:T(8,128)(2,1)}), bf16[32,16,7168]{2,1,0:T(8,128)(2,1)}, u32[]{:S(2)}, u32[]{:S(2)}) %all-to-all-start.3) | async-done | bytes 7340064 | tf_op jit(solution)/shard_map/all_to_all | solution.py:48
  585.3 6.7 %convert_reduce_fusion = f32[8,16,7168]{2,1,0:T(8,128)} fusion(bf16[32,16,7168]{2,1,0:T(8,128)(2,1)} %all-to-all-done.3), kind=kLoop, calls=%fused_computation.3 | loop fusion | flops 6422528 | bytes 11010048 | tf_op jit(solution)/shard_map/reduce_sum | solution.py:62
  592.0 5.2 gather_fusion.1
  597.2 2.3 fusion.39
  599.5 1.5 fusion.85
  (11 shorter events, 0.1 us)
Async XLA Ops:
  0.6 496.6 %copy-start = (bf16[1,7168,8]{1,2,0:T(8,128)(2,1)S(1)}, bf16[1,7168,8]{1,2,0:T(8,128)(2,1)}, u32[]{:S(2)}) copy-start(bf16[1,7168,8]{1,2,0:T(8,128)(2,1)} %param.20) | copy-start | bytes 344068
  0.6 14.7 %collective-permute-start = (bf16[1,64,7168]{2,1,0:T(8,128)(2,1)}, bf16[1,64,7168]{2,1,0:T(8,128)(2,1)S(1)}, u32[]{:S(2)}, u32[]{:S(2)}) collective-permute-start(bf16[1,64,7168]{2,1,0:T(8,128)(2,1)} %param.13), channel_id=1, source_target_pairs={{96,0},{0,32},{32,64},{64,96},{97,1},{1,33},{33,65},{65,97},{98,2}... | collective-permute-start | bytes 2752520 | tf_op jit(solution)/shard_map/ppermute | solution.py:17
  20.2 9.1 %copy-start.1 = (bf16[1,64,7168]{2,1,0:T(8,128)(2,1)S(1)}, bf16[1,64,7168]{2,1,0:T(8,128)(2,1)}, u32[]{:S(2)}) copy-start(bf16[1,64,7168]{2,1,0:T(8,128)(2,1)} %param.15) | copy-start | bytes 2752516
  20.2 9.7 %copy-start.4 = (s32[1,64,1]{1,2,0:T(1,128)S(1)}, s32[1,64,1]{1,2,0:T(1,128)}, u32[]{:S(2)}) copy-start(s32[1,64,1]{1,2,0:T(1,128)} %param.18) | copy-start | bytes 772
  20.2 101.0 %all-to-all-start = ((bf16[32,16,7168]{2,1,0:T(8,128)(2,1)}), bf16[32,16,7168]{2,1,0:T(8,128)(2,1)}, u32[]{:S(2)}, u32[]{:S(2)}) async-start(bf16[32,16,7168]{2,1,0:T(8,128)(2,1)} %bitcast.134), calls=%async_computation | async-start | bytes 14680064 | tf_op jit(solution)/shard_map/all_to_all | solution.py:56
  29.2 74.7 %collective-permute-start.1 = (bf16[1,64,7168]{2,1,0:T(8,128)(2,1)}, bf16[1,64,7168]{2,1,0:T(8,128)(2,1)S(1)}, u32[]{:S(2)}, u32[]{:S(2)}) collective-permute-start(bf16[1,64,7168]{2,1,0:T(8,128)(2,1)} %param.17), channel_id=1, source_target_pairs={{32,0},{64,32},{96,64},{0,96},{33,1},{65,33},{97,65},{1,97},{34,2}... | collective-permute-start | bytes 2752520 | tf_op jit(solution)/shard_map/ppermute | solution.py:17
  127.9 229.0 %all-to-all-start.2 = ((bf16[32,16,14336]{2,1,0:T(8,128)(2,1)}), bf16[32,16,14336]{2,1,0:T(8,128)(2,1)}, u32[]{:S(2)}, u32[]{:S(2)}) async-start(bf16[32,16,14336]{2,1,0:T(8,128)(2,1)} %bitcast.132), calls=%async_computation.2 | async-start | bytes 29360128 | tf_op jit(solution)/shard_map/all_to_all | solution.py:56
  356.8 128.3 %all-to-all-start.1 = ((bf16[32,16,7168]{2,1,0:T(8,128)(2,1)}), bf16[32,16,7168]{2,1,0:T(8,128)(2,1)}, u32[]{:S(2)}, u32[]{:S(2)}) async-start(bf16[32,16,7168]{2,1,0:T(8,128)(2,1)} %bitcast.135), calls=%async_computation.1 | async-start | bytes 14680064 | tf_op jit(solution)/shard_map/all_to_all | solution.py:48
  394.6 6.4 %copy-start.2 = (bf16[1,7168,256]{2,1,0:T(8,128)(2,1)S(1)}, bf16[1,7168,256]{2,1,0:T(8,128)(2,1)}, u32[]{:S(2)}) copy-start(bf16[1,7168,256]{2,1,0:T(8,128)(2,1)} %param.21) | copy-start | bytes 11010052
  485.2 12.5 %copy-start.5 = (s32[1,64,1]{1,2,0:T(1,128)S(1)}, s32[1,64,1]{1,2,0:T(1,128)}, u32[]{:S(2)}) copy-start(s32[1,64,1]{1,2,0:T(1,128)} %param.14) | copy-start | bytes 772
  485.2 100.1 %all-to-all-start.3 = ((bf16[32,16,7168]{2,1,0:T(8,128)(2,1)}), bf16[32,16,7168]{2,1,0:T(8,128)(2,1)}, u32[]{:S(2)}, u32[]{:S(2)}) async-start(bf16[32,16,7168]{2,1,0:T(8,128)(2,1)} %bitcast.133), calls=%async_computation.3 | async-start | bytes 14680064 | tf_op jit(solution)/shard_map/all_to_all | solution.py:48
  497.2 1.2 copy-start.3
where the time goes:
time: 609 us; the launch traced here: 601 us
  waiting for transfers between devices  412 us (68%)
  starting transfers between devices  74 us (12%)
  matrix products  72.3 us (12%)
  local copies, waits for them, and re-layouts  21 us (3%)
  other arithmetic  20.4 us (3%)
    all_to_all x2, waiting for transfers between devices, dispatch(): lax.all_to_all(copied, 'expert', split_axis=0, concat_axis=0, tiled=True)  206 us
    all_to_all x2, waiting for transfers between devices, send_back(): lax.all_to_all(partial_rows, 'expert', split_axis=0, concat_axis=0, tiled...  120 us
    ppermute x2, waiting for transfers between devices, passed_along(): return lax.ppermute(block, axis, route)  86.1 us
    all_to_all x2, starting transfers between devices, send_back(): lax.all_to_all(partial_rows, 'expert', split_axis=0, concat_axis=0, tiled...  49.7 us
    all_to_all x2, starting transfers between devices, dispatch(): lax.all_to_all(copied, 'expert', split_axis=0, concat_axis=0, tiled=True)  24.1 us
    dot_general x1, matrix products, backward_compute(): lax.dot_general(d_gate, w_gate, (((1,), (1,)), ((), ())), preferred_eleme...  18.3 us
    dot_general x1, matrix products, forward_compute(): jnp.dot(hidden, w_down, preferred_element_type=jnp.float32)  16 us
    reduce_sum x2, other arithmetic, gather_back(): jnp.sum(returned.reshape(EXPERTS, source_count // EXPERTS, slot_count, fe...  13.5 us
  transfers between devices with their start and end apart: 6, of which 6 were waited for; matrix products, arithmetic and copies ran while one was open for 14% of the time, Pallas kernels for 0%

commit v1 on v0

v1 whole, which is shorter than its diff:
```python
import functools

import jax
import jax.numpy as jnp
from jax import lax
from jax.experimental import pallas as pl
from jax.experimental.pallas import tpu as pltpu
from jax.sharding import PartitionSpec as P

MESH = pl.DeviceIdType.MESH
BF = jnp.bfloat16
F32 = jnp.float32

D = 7168
Q = 1792
T = 64
E = 8
S = 16
H = 256
ROWS = E * T
SCALE = 2.5
EPS = 1e-06
NT = (((1,), (1,)), ((), ()))
TN = (((0,), (0,)), ((), ()))

OFFS = ((1, 0), (3, 0), (0, 1), (2, 0), (1, 1), (3, 1), (2, 1))


def dot(a, b, dims=(((1,), (0,)), ((), ()))):
    return lax.dot_general(a, b, dims, preferred_element_type=F32)


def kernel(
    fwd_src, fwd_route, bwd_input, bwd_expert_out, grad_src, bwd_route, gain, router_t, gate_w, up_w, down_w,
    fwd_out, bwd_out,
    bi, arr, inc, beo, nb, nf, xb, xf, xi, sbh, sbi, rbb, rbi, rbf, rrb, rrf, fb, ff,
    wown, wn, wd, ptb, ptf, acc, ps, pr, bacc, bs, br, dgu, dgn, hid, sg, col,
    ld, pipe_s, pipe_r, pt_s, pt_r, w_s, w_r, wd_s, wd_r, xb_s, xb_r, xf_s, xf_r, xi_s, xi_r,
    yb_s, yb_r, yi_s, yi_r, yf_s, yf_r, rs_s, rs_r, bk_s, bk_r, dg_s, dg_r, hd_s, hd_r,
    qb_s, qb_r, qf_s, qf_r, fb_s, fb_r, ff_s, ff_r, out_s,
):
    p = lax.axis_index("pipe")
    ei = lax.axis_index("expert")
    me_e = ei // 4
    y, z, x = ei // 8, me_e % 2, ei % 4
    odd = x % 2

    def at_x(k):
        return (p, me_e * 4 + (x + k) % 4)

    def at_yz(k, l):
        return (p, ((y + k) % 4) * 8 + ((z + l) % 2) * 4 + x)

    def expert_at(k, l):
        return ((y + k) % 4) * 2 + (z + l) % 2

    def at_pipe(k):
        return ((p + k) % 4, ei)

    def qa(xx):
        return xx % 2

    def qb(xx):
        return 3 - xx % 2

    off_a = 1 + 2 * odd
    off_b = 3 - 2 * odd

    sends = []

    def put(src, dst, s_sem, r_sem, device):
        c = pltpu.make_async_remote_copy(
            src_ref=src, dst_ref=dst, send_sem=s_sem, recv_sem=r_sem, device_id=device, device_id_type=MESH
        )
        c.start()
        return c

    def post(*args):
        sends.append(put(*args))

    def got(ref, sem):
        pltpu.make_async_copy(ref, ref, sem).wait()

    def local(src, dst, sem):
        c = pltpu.make_async_copy(src, dst, sem)
        c.start()
        return c

    def cols(q):
        return pl.ds(pl.multiple_of(q * Q, 128), Q)

    load_bi = [local(bwd_input.at[:, pl.ds(q * Q, Q)], bi.at[q], ld.at[q]) for q in range(4)]

    barrier = pltpu.get_barrier_semaphore()
    peers = [at_x(k) for k in (1, 2, 3)] + [at_yz(k, l) for k, l in OFFS] + [at_pipe(1), at_pipe(3)]
    for peer in peers:
        pl.semaphore_signal(barrier, inc=1, device_id=peer, device_id_type=MESH)
    pl.semaphore_wait(barrier, len(peers))

    for q in range(4):
        post(grad_src.at[:, pl.ds(q * Q, Q)], inc.at[q], pipe_s.at[0, q], pipe_r.at[0, q], at_pipe(3))
    for q in range(4):
        post(fwd_src.at[:, pl.ds(q * Q, Q)], arr.at[q], pipe_s.at[1, q], pipe_r.at[1, q], at_pipe(1))

    def slots(route, table):
        chosen = route[...].astype(F32)
        lane = lax.broadcasted_iota(jnp.int32, (T, E * S), 1).astype(F32)
        hot = (lane == chosen).astype(F32)
        low = (
            lax.broadcasted_iota(jnp.int32, (T, T), 0) > lax.broadcasted_iota(jnp.int32, (T, T), 1)
        ).astype(F32)
        prior = dot(low.astype(BF), hot.astype(BF))
        rank = jnp.sum(prior * hot, axis=1, keepdims=True)
        table[0] = (lane == chosen * S + rank).astype(F32).astype(BF)

    slots(bwd_route, ptb)
    slots(fwd_route, ptf)
    for i, table in enumerate((ptb, ptf)):
        for k in (1, 2, 3):
            post(table.at[0], table.at[4 - k], pt_s.at[i, k], pt_r.at[i, 4 - k], at_x(k))

    def rms_norm(v, normed, keep):
        def rows(i, _):
            r = pl.ds(pl.multiple_of(i * 16, 16), 16)
            total = jnp.zeros((16, 1), F32)
            for q in range(4):
                w = v[q, r, :].astype(F32)
                total += jnp.sum(w * w, axis=1, keepdims=True)
            inv = lax.rsqrt(total * (1.0 / D) + EPS)
            if keep is not None:
                col[keep, r, :] = jnp.broadcast_to(inv, (16, 128))
            for q in range(4):
                normed[q, r, :] = (v[q, r, :].astype(F32) * inv * gain[q]).astype(BF)
            return 0

        lax.fori_loop(0, 4, rows, 0)

    def route_weight(normed, route, keep):
        logits = jnp.zeros((T, E), F32)
        for q in range(4):
            logits += dot(normed[q], router_t[q].astype(BF), NT)
        hot = (lax.broadcasted_iota(jnp.int32, (T, E), 1) == route[...]).astype(F32)
        weight = jax.nn.sigmoid(jnp.sum(logits * hot, axis=1, keepdims=True))
        col[keep] = jnp.broadcast_to(weight, (T, 128))

    def spread_half(normed, xs, s_sem, r_sem):
        out = []
        for j, quarter in enumerate((qa, qb)):
            local(normed.at[quarter(x)], xs.at[0, j], r_sem.at[0, j])
            for k in (1, 3, 2):
                out.append(
                    put(normed.at[quarter(x + k)], xs.at[4 - k, j], s_sem.at[k, j], r_sem.at[4 - k, j], at_x(k))
                )
        return out

    for c in load_bi:
        c.wait()
    rms_norm(bi, nb, 0)
    nb_sends = spread_half(nb, xb, xb_s, xb_r)

    for i, w in enumerate((gate_w, up_w)):
        post(w.at[qa(x + 1)], wn.at[0, i], w_s.at[0, i], w_r.at[0, i], at_x(off_a))
        post(w.at[qb(x + 1)], wn.at[1, i], w_s.at[1, i], w_r.at[1, i], at_x(off_b))
        local(w.at[qa(x)], wown.at[i, 0], ld.at[4 + 2 * i])
        local(w.at[qb(x)], wown.at[i, 1], ld.at[5 + 2 * i])

    route_weight(nb, bwd_route, 1)

    for k in (1, 2, 3):
        got(ptb.at[4 - k], pt_r.at[0, 4 - k])
        got(ptf.at[4 - k], pt_r.at[1, 4 - k])

    def place(block, table, dst):
        def one(d, _):
            r = dot(table[d], block(d)[...], TN).astype(BF).reshape(E, S, Q)
            dst[:, pl.ds(pl.multiple_of((x + d) % 4 * S, S), S), :] = r
            return 0

        return one

    def to_experts(src, dst, s_sem, r_sem):
        local(src.at[me_e], dst.at[0], r_sem(0))
        out = []
        for k, l in OFFS:
            back = ((4 - k) % 4) * 2 + l
            out.append(put(src.at[expert_at(k, l)], dst.at[back], s_sem(k * 2 + l), r_sem(back), at_yz(k, l)))
        return out

    def dispatch_half(xs, table, sb, rb, xr, ys, yr):
        out = []
        for j in range(2):
            fill = place(lambda d: xs.at[d, j], table, sb.at[j])

            def one(d, _):
                got(xs.at[d, j], xr.at[d, j])
                return fill(d, 0)

            lax.fori_loop(0, 4, one, 0)
            out += to_experts(sb.at[j], rb.at[j], lambda o: ys.at[o, j], lambda o: yr.at[o, j])
        return out

    yb_sends = dispatch_half(xb, ptb, sbh, rbb, xb_r, yb_s, yb_r)

    for q in range(4):
        got(inc.at[q], pipe_r.at[0, q])
    local(inc.at[x], xi.at[0], xi_r.at[0])
    for k in (1, 3, 2):
        post(inc.at[(x + k) % 4], xi.at[4 - k], xi_s.at[k], xi_r.at[4 - k], at_x(k))

    for q in range(4):
        got(arr.at[q], pipe_r.at[1, q])
    rms_norm(arr, nf, None)
    nf_sends = spread_half(nf, xf, xf_s, xf_r)

    local(down_w.at[:, cols(x)], wd.at[0], ld.at[8])
    for k in (1, 3, 2):
        post(down_w.at[:, cols((x + k) % 4)], wd.at[4 - k], wd_s.at[k], wd_r.at[4 - k], at_x(k))

    load_beo = [local(bwd_expert_out.at[:, pl.ds(q * Q, Q)], beo.at[q], ld.at[9 + q]) for q in range(4)]

    fill_i = place(lambda d: xi.at[d], ptb, sbi)

    def one_i(d, _):
        got(xi.at[d], xi_r.at[d])
        return fill_i(d, 0)

    lax.fori_loop(0, 4, one_i, 0)
    sends += to_experts(sbi, rbi, lambda o: yi_s.at[o], lambda o: yi_r.at[o])

    route_weight(nf, fwd_route, 2)

    for j in range(2):
        got(rbb.at[j, 0], yb_r.at[0, j])
    for c in yb_sends:
        c.wait_send()
    sends += dispatch_half(xf, ptf, sbh, rbf, xf_r, yf_s, yf_r)

    for c in load_beo:
        c.wait()

    def agree(i, _):
        r = pl.ds(pl.multiple_of(i * 16, 16), 16)
        total = jnp.zeros((16, 1), F32)
        for q in range(4):
            total += jnp.sum(inc[q, r, :].astype(F32) * beo[q, r, :].astype(F32), axis=1, keepdims=True)
        col[3, r, :] = jnp.broadcast_to(total, (16, 128))
        return 0

    lax.fori_loop(0, 4, agree, 0)

    def gate_up(rb, i):
        def one(n, _):
            w, m = n // 2, n % 2
            r = pl.ds(pl.multiple_of(m * 256, 256), 256)
            m4 = pl.ds(m * 4, 4)
            ra = rb[0, m4].reshape(256, Q)
            acc[w, r, :] = dot(ra, wown[w, 0])
            ps[i, 0, w, r, :] = dot(ra, wn[0, w]).astype(BF)
            rc = rb[1, m4].reshape(256, Q)
            acc[w, r, :] += dot(rc, wown[w, 1])
            ps[i, 1, w, r, :] = dot(rc, wn[1, w]).astype(BF)
            return 0

        lax.fori_loop(0, 4, one, 0)
        post(ps.at[i, 0], pr.at[i, 0], rs_s.at[i, 0], rs_r.at[i, 0], at_x(off_a))
        post(ps.at[i, 1], pr.at[i, 1], rs_s.at[i, 1], rs_r.at[i, 1], at_x(off_b))

    for i in range(2):
        for j in range(2):
            got(wn.at[j, i], w_r.at[j, i])
            got(wown.at[i, j], ld.at[4 + 2 * i + j])
    for j in range(2):
        for o in range(1, 8):
            got(rbb.at[j, o], yb_r.at[o, j])
    gate_up(rbb, 0)

    got(wd.at[0], ld.at[8])
    for d in (1, 2, 3):
        got(wd.at[d], wd_r.at[d])
    for o in range(8):
        got(rbi.at[o], yi_r.at[o])

    def back_own(m, _):
        r = pl.ds(pl.multiple_of(m * 256, 256), 256)
        bacc[r, :] = dot(rbi[pl.ds(m * 4, 4)].reshape(256, Q), wd[0], NT)
        return 0

    def back_other(n, _):
        d, m = 1 + n // 2, n % 2
        r = pl.ds(pl.multiple_of(m * 256, 256), 256)
        bs[d, r, :] = dot(rbi[pl.ds(m * 4, 4)].reshape(256, Q), wd[d], NT).astype(BF)
        return 0

    lax.fori_loop(0, 6, back_other, 0)
    for k in (1, 3, 2):
        post(bs.at[k], br.at[4 - k], bk_s.at[k], bk_r.at[4 - k], at_x(k))
    lax.fori_loop(0, 2, back_own, 0)

    for j in range(2):
        got(pr.at[0, j], rs_r.at[0, j])
    for d in (1, 2, 3):
        got(br.at[d], bk_r.at[d])

    def act_b(m, _):
        r = pl.ds(pl.multiple_of(m * 32, 32), 32)
        g = acc[0, r, :] + pr[0, 0, 0, r, :].astype(F32) + pr[0, 1, 0, r, :].astype(F32)
        u = acc[1, r, :] + pr[0, 0, 1, r, :].astype(F32) + pr[0, 1, 1, r, :].astype(F32)
        b = bacc[r, :] + br[1, r, :].astype(F32) + br[2, r, :].astype(F32) + br[3, r, :].astype(F32)
        s = jax.nn.sigmoid(g)
        dgu[0, r, :] = (b * u * s * (1.0 + g * (1.0 - s))).astype(BF)
        dgu[1, r, :] = (b * g * s).astype(BF)
        return 0

    lax.fori_loop(0, ROWS // 32, act_b, 0)
    post(dgu, dgn.at[0], dg_s.at[0], dg_r.at[0], at_x(off_a))
    post(dgu, dgn.at[1], dg_s.at[1], dg_r.at[1], at_x(off_b))

    for j in range(2):
        for o in range(8):
            got(rbf.at[j, o], yf_r.at[o, j])
    gate_up(rbf, 1)

    def back_home(src, dst, s_sem, r_sem):
        local(src.at[0], dst.at[me_e], r_sem(0))
        for k, l in OFFS:
            back = ((4 - k) % 4) * 2 + l
            post(src.at[k * 2 + l], dst.at[me_e], s_sem(k * 2 + l), r_sem(back), at_yz(k, l))

    for j in range(2):
        got(dgn.at[j], dg_r.at[j])

        def cols_b(n, _):
            c = pl.ds(pl.multiple_of(n * 256, 256), 256)
            r = dot(dgu[0], wown[0, j, c, :], NT)
            r += dot(dgu[1], wown[1, j, c, :], NT)
            r += dot(dgn[j, 0], wn[j, 0, c, :], NT)
            r += dot(dgn[j, 1], wn[j, 1, c, :], NT)
            rbb[j, :, :, c] = r.astype(BF).reshape(E, T, 256)
            return 0

        lax.fori_loop(0, Q // 256, cols_b, 0)
        back_home(rbb.at[j], rrb.at[j], lambda o: qb_s.at[o, j], lambda o: qb_r.at[o, j])

    for j in range(2):
        got(pr.at[1, j], rs_r.at[1, j])

    def act_f(m, _):
        r = pl.ds(pl.multiple_of(m * 32, 32), 32)
        g = acc[0, r, :] + pr[1, 0, 0, r, :].astype(F32) + pr[1, 1, 0, r, :].astype(F32)
        u = acc[1, r, :] + pr[1, 0, 1, r, :].astype(F32) + pr[1, 1, 1, r, :].astype(F32)
        hid[0, r, :] = (g * jax.nn.sigmoid(g) * u).astype(BF)
        return 0

    lax.fori_loop(0, ROWS // 32, act_f, 0)
    for k in (1, 3, 2):
        post(hid.at[0], hid.at[4 - k], hd_s.at[k], hd_r.at[4 - k], at_x(k))
    for d in (1, 2, 3):
        got(hid.at[d], hd_r.at[d])

    def cols_f(n, _):
        c = pl.ds(pl.multiple_of(n * 256, 256), 256)
        r = dot(hid[0], wd[0, :, c])
        for d in (1, 2, 3):
            r += dot(hid[d], wd[d, :, c])
        rbi[:, :, c] = r.astype(BF).reshape(E, T, 256)
        return 0

    lax.fori_loop(0, Q // 256, cols_f, 0)
    back_home(rbi, rrf, lambda o: qf_s.at[o], lambda o: qf_r.at[o])

    def unplace(src, table, dst):
        def one(d, _):
            rows = src[:, pl.ds(pl.multiple_of((x + d) % 4 * S, S), S), :].reshape(E * S, Q)
            dst(d)[...] = dot(table[d], rows).astype(BF)
            return 0

        lax.fori_loop(0, 4, one, 0)

    for j in range(2):
        for o in range(8):
            got(rrb.at[j, 0], qb_r.at[o, j])
        unplace(rrb.at[j], ptb, lambda d: xb.at[d, j])
        for k in (1, 3, 2):
            post(xb.at[k, j], fb.at[4 - k, j], fb_s.at[k, j], fb_r.at[4 - k, j], at_x(k))

    for o in range(8):
        got(rrf.at[0], qf_r.at[o])
    unplace(rrf, ptf, lambda d: xi.at[d])
    for k in (1, 3, 2):
        post(xi.at[k], ff.at[4 - k], ff_s.at[k], ff_r.at[4 - k], at_x(k))

    for c in nb_sends + nf_sends:
        c.wait_send()
    for j in range(2):
        for d in (1, 2, 3):
            got(fb.at[d, j], fb_r.at[d, j])
    quarters = ((qa(x), 0, 0), (qb(x), 0, 1), (qa(x + 1), 1, 0), (qb(x + 1), 1, 1))

    def finish_b(i, _):
        r = pl.ds(pl.multiple_of(i * 16, 16), 16)
        inv = col[0, r, 0:1]
        weight = col[1, r, 0:1]
        d_logit = SCALE * col[3, r, 0:1] * weight * (1.0 - weight)
        hot = (lax.broadcasted_iota(jnp.int32, (16, E), 1) == bwd_route[r, :]).astype(BF)
        total = jnp.zeros((16, 1), F32)
        for q, other, j in quarters:
            if other:
                g = fb[1, j, r, :].astype(F32) + fb[3, j, r, :].astype(F32)
            else:
                g = xb[0, j, r, :].astype(F32) + fb[2, j, r, :].astype(F32)
            dn = SCALE * weight * g + d_logit * dot(hot, router_t[q].astype(BF))
            s = dn * gain[q]
            sg[q, r, :] = s
            total += jnp.sum(s * bi[q, r, :].astype(F32), axis=1, keepdims=True)
        factor = inv * inv * inv * (total * (1.0 / D))
        for q in range(4):
            v = bi[q, r, :].astype(F32)
            o = inc[q, r, :].astype(F32) + (inv * sg[q, r, :] - v * factor)
            nb[q, r, :] = o.astype(BF)
        return 0

    lax.fori_loop(0, 4, finish_b, 0)
    outs = [local(nb.at[q], bwd_out.at[:, pl.ds(q * Q, Q)], out_s.at[0, q]) for q in range(4)]

    for d in (1, 2, 3):
        got(ff.at[d], ff_r.at[d])

    def finish_f(i, _):
        r = pl.ds(pl.multiple_of(i * 16, 16), 16)
        weight = col[2, r, 0:1]
        for d in range(4):
            q = (x + d) % 4
            e = (xi[0, r, :] if d == 0 else ff[d, r, :]).astype(F32)
            nf[q, r, :] = (arr[q, r, :].astype(F32) + SCALE * weight * e).astype(BF)
        return 0

    lax.fori_loop(0, 4, finish_f, 0)
    outs += [local(nf.at[q], fwd_out.at[:, pl.ds(q * Q, Q)], out_s.at[1, q]) for q in range(4)]

    for c in sends:
        c.wait_send()
    for c in outs:
        c.wait()


def shards(
    fwd_src, fwd_route, bwd_input, bwd_expert_out, grad_src, bwd_route, norm_gain, router, gate_w, up_w, down_w
):
    gain = norm_gain[0].astype(F32).reshape(4, 1, Q)
    router_t = router[0].T.astype(F32).reshape(E, 4, Q).transpose(1, 0, 2)
    hbm = pl.BlockSpec(memory_space=pl.ANY)
    vmem = pl.BlockSpec(memory_space=pltpu.VMEM)
    dma = pltpu.SemaphoreType.DMA

    def buf(*shape, dtype=BF):
        return pltpu.VMEM(shape, dtype)

    scratch = [
        buf(4, T, Q), buf(4, T, Q), buf(4, T, Q), buf(4, T, Q),
        buf(4, T, Q), buf(4, T, Q),
        buf(4, 2, T, Q), buf(4, 2, T, Q), buf(4, T, Q),
        buf(2, E, T, Q), buf(E, T, Q),
        buf(2, E, T, Q), buf(E, T, Q), buf(2, E, T, Q),
        buf(2, E, T, Q), buf(E, T, Q),
        buf(4, 2, T, Q), buf(4, T, Q),
        buf(2, 2, Q, H), buf(2, 2, Q, H), buf(4, H, Q),
        buf(4, T, E * S), buf(4, T, E * S),
        buf(2, ROWS, H, dtype=F32), buf(2, 2, 2, ROWS, H), buf(2, 2, 2, ROWS, H),
        buf(ROWS, H, dtype=F32), buf(4, ROWS, H), buf(4, ROWS, H),
        buf(2, ROWS, H), buf(2, 2, ROWS, H), buf(4, ROWS, H),
        buf(4, T, Q, dtype=F32), buf(4, T, 128, dtype=F32),
        dma((16,)), dma((2, 4)), dma((2, 4)), dma((2, 4)), dma((2, 4)),
        dma((2, 2)), dma((2, 2)), dma((4,)), dma((4,)),
        dma((4, 2)), dma((4, 2)), dma((4, 2)), dma((4, 2)), dma((4,)), dma((4,)),
        dma((8, 2)), dma((8, 2)), dma((8,)), dma((8,)), dma((8, 2)), dma((8, 2)),
        dma((2, 2)), dma((2, 2)), dma((4,)), dma((4,)), dma((2,)), dma((2,)), dma((4,)), dma((4,)),
        dma((8, 2)), dma((8, 2)), dma((8,)), dma((8,)),
        dma((4, 2)), dma((4, 2)), dma((4,)), dma((4,)), dma((2, 4)),
    ]
    out = jax.ShapeDtypeStruct((T, D), BF)
    fwd_out, bwd_out = pl.pallas_call(
        kernel,
        out_shape=(out, out),
        in_specs=[hbm, vmem, hbm, hbm, hbm, vmem, vmem, vmem, hbm, hbm, hbm],
        out_specs=(hbm, hbm),
        scratch_shapes=scratch,
        compiler_params=pltpu.CompilerParams(
            collective_id=0, has_side_effects=True, vmem_limit_bytes=62 * 1024 * 1024
        ),
        cost_estimate=pl.CostEstimate(
            flops=15_000_000_000, bytes_accessed=20_000_000, transcendentals=400_000
        ),
    )(
        fwd_src[0],
        fwd_route[0],
        bwd_input[0],
        bwd_expert_out[0],
        grad_src[0],
        bwd_route[0],
        gain,
        router_t,
        gate_w[0].reshape(4, Q, H),
        up_w[0].reshape(4, Q, H),
        down_w[0],
    )
    return (fwd_out[None], bwd_out[None])


def solution(mesh):
    placed = (
        P("pipe", "expert", None),
        P("pipe", "expert", None),
        P("pipe", "expert", None),
        P("pipe", "expert", None),
        P("pipe", "expert", None),
        P("pipe", "expert", None),
        P("pipe", None),
        P("pipe", None, None),
        P("pipe", None, "expert"),
        P("pipe", None, "expert"),
        P("pipe", "expert", None),
    )
    return jax.shard_map(
        shards,
        mesh=mesh,
        in_specs=placed,
        out_specs=(P("pipe", "expert", None), P("pipe", "expert", None)),
        check_vma=False,
    )
```

time: 609 us -> 275 us (0.45); the launches traced: 601 us -> 275 us
  waiting for transfers between devices: 412 us -> 0 us
  Pallas kernels: 0 us -> 264 us
  starting transfers between devices: 74 us -> 0 us
  matrix products: 72.3 us -> 0 us
  other arithmetic: 20.4 us -> 2.99 us
  local copies, waits for them, and re-layouts: 21 us -> 7.03 us
    all_to_all x4 -> x0, waiting for transfers between devices: 326 us -> none  [the longest x2 206 us: dispatch(): lax.all_to_all(copied, 'expert', split_axis=0, concat_axis=0, tiled=True)]
    pallas_call x0 -> x1, Pallas kernels: none -> 264 us  [shards(): pl.pallas_call(kernel, out_shape=(out, out), in_specs=[hbm, vmem, hbm, hb...]
    ppermute x2 -> x0, waiting for transfers between devices: 86.1 us -> none  [passed_along(): return lax.ppermute(block, axis, route)]
    all_to_all x4 -> x0, starting transfers between devices: 73.9 us -> none  [the longest x2 49.7 us: send_back(): lax.all_to_all(partial_rows, 'expert', split_axis=0, concat_axis=0, tiled...]
    dot_general x13 -> x0, matrix products: 72.3 us -> none  [the longest x1 18.3 us: backward_compute(): lax.dot_general(d_gate, w_gate, (((1,), (1,)), ((), ())), preferred_eleme...]
    reduce_sum x5 -> x0, other arithmetic: 14.4 us -> none  [the longest x2 13.5 us: gather_back(): jnp.sum(returned.reshape(EXPERTS, source_count // EXPERTS, slot_count, fe...]
    broadcast_in_dim x2 -> x0, local copies, waits for them, and re-layouts: 10.5 us -> none  [dispatch(): jnp.broadcast_to(bundle[:, None], (bundle.shape[0], shard_count) + bundle...]
    gather x2 -> x0, local copies, waits for them, and re-layouts: 10.3 us -> none  [gather_back(): return jnp.take(flat_rows, slot_index, axis=0)]
  transfers between devices with their start and end apart: 6 -> 0, of which waited for: 6 -> 0; matrix products, arithmetic and copies ran while one was open for 14% -> 0% of each run, Pallas kernels for 0% -> 0%
where the time goes in v1:
time: 275 us
  Pallas kernels  264 us (96%)
  local copies, waits for them, and re-layouts  7.03 us (3%)
  other arithmetic  2.99 us (1%)
    pallas_call x1, Pallas kernels, shards(): pl.pallas_call(kernel, out_shape=(out, out), in_specs=[hbm, vmem, hbm, hb...  264 us

profile of v1, /device:TPU:8, one launch (start us, length us, event | category | flops | bytes accessed | tf_op | source)
XLA Modules:
  0.0 274.7 jit_solution(2847359958248850514)
XLA Ops:
  0.6 1.4 convert.5.gain
  2.0 1.4 copy.13.fwd_route
  3.4 1.4 copy.14.bwd_route
  4.7 1.6 bitcast_convert_fusion
  6.3 264.0 %shard_map.122 = (bf16[64,7168]{1,0:T(8,128)(2,1)}, bf16[64,7168]{1,0:T(8,128)(2,1)}) custom-call(bf16[64,7168]{1,0:T(8,128)(2,1)} %bitcast.30, s32[64,1]{1,0:T(8,128)} %copy.13.fwd_route, bf16[64,7168]{1,0:T(8,128)(2,1)} %bitcast.31, bf16[64,7168]{1,0:T(8,128)(2,1)} %bitcast.32, bf16[64,7168]{1,0:T(8,128)(2,1)} %bitcast.33, s32[64,1]{1,0:T(8,128)} %copy.14.bwd_route, ...), custom_call_target="tpu_custom_call" | custom-call | flops 15000000512 | bytes 20000000 | tf_op jit(solution)/shard_map/pallas_call | solution.py:481
  270.3 2.2 copy.17
  272.5 2.2 copy.18

commit v2 on v1

v2 whole, which is shorter than its diff:
```python
import functools

import jax
import jax.numpy as jnp
from jax import lax
from jax.experimental import pallas as pl
from jax.experimental.pallas import tpu as pltpu
from jax.sharding import PartitionSpec as P

MESH = pl.DeviceIdType.MESH
BF = jnp.bfloat16
F32 = jnp.float32

D = 7168
Q = 1792
T = 64
E = 8
S = 16
H = 256
ROWS = E * T
SCALE = 2.5
EPS = 1e-06
NT = (((1,), (1,)), ((), ()))
TN = (((0,), (0,)), ((), ()))

OFFS = ((1, 0), (3, 0), (0, 1), (2, 0), (1, 1), (3, 1), (2, 1))


def dot(a, b, dims=(((1,), (0,)), ((), ()))):
    return lax.dot_general(a, b, dims, preferred_element_type=F32)


def kernel(
    fwd_src, fwd_route, bwd_input, bwd_expert_out, grad_src, bwd_route, gain_row, router_t, gate_w, up_w, down_w,
    fwd_out, bwd_out,
    bi, arr, inc, beo, nb, nf, xb, xf, xi, sbh, sbi, rbb, rbi, rbf, rrb, rrf, rrc, gb, gs, fb, ff,
    wown, wn, wd, ptb, ptf, acc, ps, pr, bacc, bs, br, dgu, dgn, hid, sg, col, gain,
    ld, pipe_s, pipe_r, pt_s, pt_r, w_s, w_r, wd_s, wd_r, xb_s, xb_r, xf_s, xf_r, xi_s, xi_r,
    yb_s, yb_r, yi_s, yi_r, yf_s, yf_r, rs_s, rs_r, bk_s, bk_r, dg_s, dg_r, hd_s, hd_r,
    gb_s, gb_r, qb_s, qb_r, qc_s, qc_r, qf_s, qf_r, fb_s, fb_r, ff_s, ff_r, out_s,
):
    p = lax.axis_index("pipe")
    ei = lax.axis_index("expert")
    me_e = ei // 4
    y, z, x = ei // 8, me_e % 2, ei % 4
    odd = x % 2

    def at_x(k):
        return (p, me_e * 4 + (x + k) % 4)

    def at_yz(k, l):
        return (p, ((y + k) % 4) * 8 + ((z + l) % 2) * 4 + x)

    def expert_at(k, l):
        return ((y + k) % 4) * 2 + (z + l) % 2

    def at_pipe(k):
        return ((p + k) % 4, ei)

    def qa(xx):
        return xx % 2

    def qb(xx):
        return 3 - xx % 2

    off_a = 1 + 2 * odd
    off_b = 3 - 2 * odd

    sends = []

    def put(src, dst, s_sem, r_sem, device):
        c = pltpu.make_async_remote_copy(
            src_ref=src, dst_ref=dst, send_sem=s_sem, recv_sem=r_sem, device_id=device, device_id_type=MESH
        )
        c.start()
        return c

    def post(*args):
        sends.append(put(*args))

    def got(ref, sem):
        pltpu.make_async_copy(ref, ref, sem).wait()

    def local(src, dst, sem):
        c = pltpu.make_async_copy(src, dst, sem)
        c.start()
        return c

    def cols(q):
        return pl.ds(pl.multiple_of(q * Q, 128), Q)

    load_bi = [local(bwd_input.at[:, pl.ds(q * Q, Q)], bi.at[q], ld.at[q]) for q in range(4)]

    barrier = pltpu.get_barrier_semaphore()
    peers = [at_x(k) for k in (1, 2, 3)] + [at_yz(k, l) for k, l in OFFS] + [at_pipe(1), at_pipe(3)]
    for peer in peers:
        pl.semaphore_signal(barrier, inc=1, device_id=peer, device_id_type=MESH)
    pl.semaphore_wait(barrier, len(peers))

    def swap_weights(i, w):
        post(w.at[qa(x + 1)], wn.at[0, i], w_s.at[0, i], w_r.at[0, i], at_x(off_a))
        post(w.at[qb(x + 1)], wn.at[1, i], w_s.at[1, i], w_r.at[1, i], at_x(off_b))

    def slots(route, table, keep):
        row = lax.broadcasted_iota(jnp.int32, (T, T), 0)
        lower = lax.broadcasted_iota(jnp.int32, (T, T), 1)
        eye = (row == lower).astype(F32)
        chosen = jnp.sum(eye * route[...].astype(F32), axis=1, keepdims=True)
        col[keep] = jnp.broadcast_to(chosen, (T, 128))
        lane = lax.broadcasted_iota(jnp.int32, (T, E * S), 1).astype(F32)
        hot = (lane == chosen).astype(F32)
        low = (row > lower).astype(F32)
        prior = dot(low.astype(BF), hot.astype(BF))
        rank = jnp.sum(prior * hot, axis=1, keepdims=True)
        table[0] = (lane == chosen * S + rank).astype(F32).astype(BF)

    slots(bwd_route, ptb, 4)
    slots(fwd_route, ptf, 5)
    for i, table in enumerate((ptb, ptf)):
        for k in (1, 2, 3):
            post(table.at[0], table.at[4 - k], pt_s.at[i, k], pt_r.at[i, 4 - k], at_x(k))

    def rms_norm(v, normed, keep):
        def rows(i, _):
            r = pl.ds(pl.multiple_of(i * 16, 16), 16)
            total = jnp.zeros((16, 1), F32)
            for q in range(4):
                w = v[q, r, :].astype(F32)
                total += jnp.sum(w * w, axis=1, keepdims=True)
            inv = lax.rsqrt(total * (1.0 / D) + EPS)
            if keep is not None:
                col[keep, r, :] = jnp.broadcast_to(inv, (16, 128))
            for q in range(4):
                normed[q, r, :] = (v[q, r, :].astype(F32) * inv * gain[q]).astype(BF)
            return 0

        lax.fori_loop(0, 4, rows, 0)

    def route_weight(normed, chosen, keep):
        logits = jnp.zeros((T, E), F32)
        for q in range(4):
            logits += dot(normed[q], router_t[:, q * Q : (q + 1) * Q], NT)
        hot = (lax.broadcasted_iota(jnp.int32, (T, E), 1).astype(F32) == col[chosen, :, 0:1]).astype(F32)
        weight = jax.nn.sigmoid(jnp.sum(logits * hot, axis=1, keepdims=True))
        col[keep] = jnp.broadcast_to(weight, (T, 128))

    def spread_half(j, normed, xs, s_sem, r_sem):
        quarter = (qa, qb)[j]
        local(normed.at[quarter(x)], xs.at[0, j], r_sem.at[0, j])
        return [
            put(normed.at[quarter(x + k)], xs.at[4 - k, j], s_sem.at[k, j], r_sem.at[4 - k, j], at_x(k))
            for k in (1, 3, 2)
        ]

    def place(block, table, dst):
        def one(d, _):
            r = dot(table[d], block(d)[...], TN).astype(BF).reshape(E, S, Q)
            dst[:, pl.ds(pl.multiple_of((x + d) % 4 * S, S), S), :] = r
            return 0

        return one

    def to_experts(src, dst, s_sem, r_sem):
        local(src.at[me_e], dst.at[0], r_sem(0))
        out = []
        for k, l in OFFS:
            back = ((4 - k) % 4) * 2 + l
            out.append(put(src.at[expert_at(k, l)], dst.at[back], s_sem(k * 2 + l), r_sem(back), at_yz(k, l)))
        return out

    def dispatch_half(j, xs, table, sb, rb, xr, ys, yr):
        fill = place(lambda d: xs.at[d, j], table, sb.at[j])

        def one(d, _):
            got(xs.at[d, j], xr.at[d, j])
            return fill(d, 0)

        lax.fori_loop(0, 4, one, 0)
        return to_experts(sb.at[j], rb.at[j], lambda o: ys.at[o, j], lambda o: yr.at[o, j])

    def gate_up(rb, i):
        def one(n, _):
            w, m = n // 2, n % 2
            r = pl.ds(pl.multiple_of(m * 256, 256), 256)
            m4 = pl.ds(m * 4, 4)
            ra = rb[0, m4].reshape(256, Q)
            acc[i, w, r, :] = dot(ra, wown[w, 0])
            ps[i, 0, w, r, :] = dot(ra, wn[0, w]).astype(BF)
            rc = rb[1, m4].reshape(256, Q)
            acc[i, w, r, :] += dot(rc, wown[w, 1])
            ps[i, 1, w, r, :] = dot(rc, wn[1, w]).astype(BF)
            return 0

        lax.fori_loop(0, 4, one, 0)

    def swap_parts(i):
        post(ps.at[i, 0], pr.at[i, 0], rs_s.at[i, 0], rs_r.at[i, 0], at_x(off_a))
        post(ps.at[i, 1], pr.at[i, 1], rs_s.at[i, 1], rs_r.at[i, 1], at_x(off_b))

    def back_home(src, dst, s_sem, r_sem):
        local(src.at[0], dst.at[me_e], r_sem(0))
        for k, l in OFFS:
            back = ((4 - k) % 4) * 2 + l
            post(src.at[k * 2 + l], dst.at[me_e], s_sem(k * 2 + l), r_sem(back), at_yz(k, l))

    def input_part(j):
        got(dgn.at[j], dg_r.at[j])

        def cols_b(n, _):
            c = pl.ds(pl.multiple_of(n * 256, 256), 256)
            r = dot(dgu[0], wown[0, j, c, :], NT)
            r += dot(dgu[1], wown[1, j, c, :], NT)
            r += dot(dgn[j, 0], wn[j, 0, c, :], NT)
            r += dot(dgn[j, 1], wn[j, 1, c, :], NT)
            rbb[j, :, :, c] = r.astype(BF).reshape(E, T, 256)
            return 0

        lax.fori_loop(0, Q // 256, cols_b, 0)

    def slot_rows(k):
        return pl.ds(pl.multiple_of((x + k) % 4 * S, S), S)

    def unplace(src, table, dst):
        def one(d, _):
            rows = src[:, pl.ds(pl.multiple_of((x + d) % 4 * S, S), S), :].reshape(E * S, Q)
            dst(d)[...] = dot(table[d], rows).astype(BF)
            return 0

        lax.fori_loop(0, 4, one, 0)

    outs = []
    swap_weights(0, gate_w)
    for q in range(4):
        post(fwd_src.at[:, pl.ds(q * Q, Q)], arr.at[q], pipe_s.at[1, q], pipe_r.at[1, q], at_pipe(1))
    for q in range(4):
        post(grad_src.at[:, pl.ds(q * Q, Q)], inc.at[q], pipe_s.at[0, q], pipe_r.at[0, q], at_pipe(3))

    for q in range(4):
        gain[q] = gain_row[:, q * Q : (q + 1) * Q].astype(F32)
    for c in load_bi:
        c.wait()
    rms_norm(bi, nb, 0)
    nb_sends = spread_half(0, nb, xb, xb_s, xb_r)
    nb_sends += spread_half(1, nb, xb, xb_s, xb_r)
    swap_weights(1, up_w)
    for i, w in enumerate((gate_w, up_w)):
        local(w.at[qa(x)], wown.at[i, 0], ld.at[4 + 2 * i])
        local(w.at[qb(x)], wown.at[i, 1], ld.at[5 + 2 * i])
    load_beo = [local(bwd_expert_out.at[:, pl.ds(q * Q, Q)], beo.at[q], ld.at[9 + q]) for q in range(4)]
    local(down_w.at[:, cols(x)], wd.at[0], ld.at[8])

    route_weight(nb, 4, 1)

    for k in (1, 2, 3):
        got(ptb.at[4 - k], pt_r.at[0, 4 - k])
        got(ptf.at[4 - k], pt_r.at[1, 4 - k])

    yb_sends = [dispatch_half(0, xb, ptb, sbh, rbb, xb_r, yb_s, yb_r)]
    yb_sends.append(dispatch_half(1, xb, ptb, sbh, rbb, xb_r, yb_s, yb_r))
    for q in range(4):
        got(arr.at[q], pipe_r.at[1, q])
    rms_norm(arr, nf, None)
    nf_sends = spread_half(0, nf, xf, xf_s, xf_r) + spread_half(1, nf, xf, xf_s, xf_r)
    for q in range(4):
        got(inc.at[q], pipe_r.at[0, q])
    local(inc.at[x], xi.at[0], xi_r.at[0])
    for k in (1, 3, 2):
        post(inc.at[(x + k) % 4], xi.at[4 - k], xi_s.at[k], xi_r.at[4 - k], at_x(k))

    for k in (1, 3, 2):
        post(down_w.at[:, cols((x + k) % 4)], wd.at[4 - k], wd_s.at[k], wd_r.at[4 - k], at_x(k))

    for c in load_beo:
        c.wait()

    def agree(i, _):
        r = pl.ds(pl.multiple_of(i * 16, 16), 16)
        total = jnp.zeros((16, 1), F32)
        for q in range(4):
            total += jnp.sum(inc[q, r, :].astype(F32) * beo[q, r, :].astype(F32), axis=1, keepdims=True)
        col[3, r, :] = jnp.broadcast_to(total, (16, 128))
        return 0

    lax.fori_loop(0, 4, agree, 0)

    route_weight(nf, 5, 2)

    got(rbb.at[0, 0], yb_r.at[0, 0])
    for c in yb_sends[0]:
        c.wait_send()
    sends += dispatch_half(0, xf, ptf, sbh, rbf, xf_r, yf_s, yf_r)

    got(rbb.at[1, 0], yb_r.at[0, 1])
    for c in yb_sends[1]:
        c.wait_send()
    sends += dispatch_half(1, xf, ptf, sbh, rbf, xf_r, yf_s, yf_r)

    fill_i = place(lambda d: xi.at[d], ptb, sbi)

    def one_i(d, _):
        got(xi.at[d], xi_r.at[d])
        return fill_i(d, 0)

    lax.fori_loop(0, 4, one_i, 0)
    sends += to_experts(sbi, rbi, lambda o: yi_s.at[o], lambda o: yi_r.at[o])

    for i in range(2):
        for j in range(2):
            got(wn.at[j, i], w_r.at[j, i])
            got(wown.at[i, j], ld.at[4 + 2 * i + j])
    for j in range(2):
        for o in range(1, 8):
            got(rbb.at[j, o], yb_r.at[o, j])
    gate_up(rbb, 0)


    swap_parts(0)
    for j in range(2):
        for o in range(8):
            got(rbf.at[j, o], yf_r.at[o, j])
    gate_up(rbf, 1)
    swap_parts(1)
    for j in range(2):
        got(pr.at[1, j], rs_r.at[1, j])

    def act_f(m, _):
        r = pl.ds(pl.multiple_of(m * 32, 32), 32)
        g = acc[1, 0, r, :] + pr[1, 0, 0, r, :].astype(F32) + pr[1, 1, 0, r, :].astype(F32)
        u = acc[1, 1, r, :] + pr[1, 0, 1, r, :].astype(F32) + pr[1, 1, 1, r, :].astype(F32)
        hid[0, r, :] = (g * jax.nn.sigmoid(g) * u).astype(BF)
        return 0

    lax.fori_loop(0, ROWS // 32, act_f, 0)
    for k in (1, 3, 2):
        post(hid.at[0], hid.at[4 - k], hd_s.at[k], hd_r.at[4 - k], at_x(k))

    got(wd.at[0], ld.at[8])
    for d in (1, 2, 3):
        got(wd.at[d], wd_r.at[d])
    for o in range(8):
        got(rbi.at[o], yi_r.at[o])

    def back_own(m, _):
        r = pl.ds(pl.multiple_of(m * 256, 256), 256)
        bacc[r, :] = dot(rbi[pl.ds(m * 4, 4)].reshape(256, Q), wd[0], NT)
        return 0

    def back_other(n, _):
        d, m = 1 + n // 2, n % 2
        r = pl.ds(pl.multiple_of(m * 256, 256), 256)
        bs[d, r, :] = dot(rbi[pl.ds(m * 4, 4)].reshape(256, Q), wd[d], NT).astype(BF)
        return 0

    lax.fori_loop(0, 6, back_other, 0)
    for k in (1, 3, 2):
        post(bs.at[k], br.at[4 - k], bk_s.at[k], bk_r.at[4 - k], at_x(k))
    lax.fori_loop(0, 2, back_own, 0)

    for d in (1, 2, 3):
        got(hid.at[d], hd_r.at[d])

    def cols_f(n, _):
        c = pl.ds(pl.multiple_of(n * 256, 256), 256)
        r = dot(hid[0], wd[0, :, c])
        for d in (1, 2, 3):
            r += dot(hid[d], wd[d, :, c])
        rbi[:, :, c] = r.astype(BF).reshape(E, T, 256)
        return 0

    lax.fori_loop(0, Q // 256, cols_f, 0)
    back_home(rbi, rrf, lambda o: qf_s.at[o], lambda o: qf_r.at[o])

    for j in range(2):
        got(pr.at[0, j], rs_r.at[0, j])
    for d in (1, 2, 3):
        got(br.at[d], bk_r.at[d])

    def act_b(m, _):
        r = pl.ds(pl.multiple_of(m * 32, 32), 32)
        g = acc[0, 0, r, :] + pr[0, 0, 0, r, :].astype(F32) + pr[0, 1, 0, r, :].astype(F32)
        u = acc[0, 1, r, :] + pr[0, 0, 1, r, :].astype(F32) + pr[0, 1, 1, r, :].astype(F32)
        b = bacc[r, :] + br[1, r, :].astype(F32) + br[2, r, :].astype(F32) + br[3, r, :].astype(F32)
        s = jax.nn.sigmoid(g)
        dgu[0, r, :] = (b * u * s * (1.0 + g * (1.0 - s))).astype(BF)
        dgu[1, r, :] = (b * g * s).astype(BF)
        return 0

    lax.fori_loop(0, ROWS // 32, act_b, 0)
    post(dgu, dgn.at[0], dg_s.at[0], dg_r.at[0], at_x(off_a))
    post(dgu, dgn.at[1], dg_s.at[1], dg_r.at[1], at_x(off_b))

    input_part(1)
    for k in (1, 3, 2):
        post(rbb.at[1, :, slot_rows(k)], gb.at[4 - k], gb_s.at[k], gb_r.at[4 - k], at_x(k))
    input_part(0)
    back_home(rbb.at[0], rrb, lambda o: qb_s.at[o], lambda o: qb_r.at[o])

    for o in range(8):
        got(rrf.at[0], qf_r.at[o])
    unplace(rrf, ptf, lambda d: xi.at[d])
    for k in (1, 3, 2):
        post(xi.at[k], ff.at[4 - k], ff_s.at[k], ff_r.at[4 - k], at_x(k))

    for d in (1, 2, 3):
        got(gb.at[d], gb_r.at[d])

    def sum_b(o, _):
        own = rbb[1, o, slot_rows(0), :].astype(F32)
        gs[o, 0] = (own + gb[2, o].astype(F32)).astype(BF)
        gs[o, 1] = (gb[1, o].astype(F32) + gb[3, o].astype(F32)).astype(BF)
        return 0

    lax.fori_loop(0, E, sum_b, 0)
    back_home(gs, rrc, lambda o: qc_s.at[o], lambda o: qc_r.at[o])

    for o in range(8):
        got(rrb.at[0], qb_r.at[o])
    unplace(rrb, ptb, lambda d: xb.at[d, 0])
    for k in (1, 3, 2):
        post(xb.at[k, 0], fb.at[4 - k], fb_s.at[k], fb_r.at[4 - k], at_x(k))

    for c in nf_sends:
        c.wait_send()
    for d in (1, 2, 3):
        got(ff.at[d], ff_r.at[d])

    def finish_f(i, _):
        r = pl.ds(pl.multiple_of(i * 16, 16), 16)
        weight = col[2, r, 0:1]
        for d in range(4):
            q = (x + d) % 4
            e = (xi[0, r, :] if d == 0 else ff[d, r, :]).astype(F32)
            nf[q, r, :] = (arr[q, r, :].astype(F32) + SCALE * weight * e).astype(BF)
        return 0

    lax.fori_loop(0, 4, finish_f, 0)
    outs += [local(nf.at[q], fwd_out.at[:, pl.ds(q * Q, Q)], out_s.at[1, q]) for q in range(4)]

    for c in nb_sends:
        c.wait_send()
    for o in range(8):
        got(rrc.at[0], qc_r.at[o])
    for j in range(2):
        xb[j, 1] = dot(ptb[0], rrc[:, j].reshape(E * S, Q)).astype(BF)
    for d in (1, 2, 3):
        got(fb.at[d], fb_r.at[d])
    quarters = (
        (qa(x), lambda r: xb[0, 0, r, :].astype(F32) + fb[2, r, :].astype(F32)),
        (qa(x + 1), lambda r: fb[1, r, :].astype(F32) + fb[3, r, :].astype(F32)),
        (qb(x), lambda r: xb[0, 1, r, :].astype(F32)),
        (qb(x + 1), lambda r: xb[1, 1, r, :].astype(F32)),
    )

    def finish_b(i, _):
        r = pl.ds(pl.multiple_of(i * 16, 16), 16)
        inv = col[0, r, 0:1]
        weight = col[1, r, 0:1]
        d_logit = SCALE * col[3, r, 0:1] * weight * (1.0 - weight)
        hot = (lax.broadcasted_iota(jnp.int32, (16, E), 1).astype(F32) == col[4, r, 0:1]).astype(F32).astype(BF)
        total = jnp.zeros((16, 1), F32)
        for q, part in quarters:
            g = part(r)
            dn = SCALE * weight * g + d_logit * dot(hot, router_t[:, cols(q)])
            s = dn * gain[q]
            sg[q, r, :] = s
            total += jnp.sum(s * bi[q, r, :].astype(F32), axis=1, keepdims=True)
        factor = inv * inv * inv * (total * (1.0 / D))
        for q in range(4):
            v = bi[q, r, :].astype(F32)
            o = inc[q, r, :].astype(F32) + (inv * sg[q, r, :] - v * factor)
            nb[q, r, :] = o.astype(BF)
        return 0

    lax.fori_loop(0, 4, finish_b, 0)
    outs += [local(nb.at[q], bwd_out.at[:, pl.ds(q * Q, Q)], out_s.at[0, q]) for q in range(4)]

    for c in sends:
        c.wait_send()
    for c in outs:
        c.wait()


def shards(
    fwd_src, fwd_route, bwd_input, bwd_expert_out, grad_src, bwd_route, norm_gain, router, gate_w, up_w, down_w
):
    hbm = pl.BlockSpec(memory_space=pl.ANY)
    vmem = pl.BlockSpec(memory_space=pltpu.VMEM)
    dma = pltpu.SemaphoreType.DMA

    def buf(*shape, dtype=BF):
        return pltpu.VMEM(shape, dtype)

    scratch = [
        buf(4, T, Q), buf(4, T, Q), buf(4, T, Q), buf(4, T, Q),
        buf(4, T, Q), buf(4, T, Q),
        buf(4, 2, T, Q), buf(4, 2, T, Q), buf(4, T, Q),
        buf(2, E, T, Q), buf(E, T, Q),
        buf(2, E, T, Q), buf(E, T, Q), buf(2, E, T, Q),
        buf(E, T, Q), buf(E, T, Q), buf(E, 2, S, Q),
        buf(4, E, S, Q), buf(E, 2, S, Q),
        buf(4, T, Q), buf(4, T, Q),
        buf(2, 2, Q, H), buf(2, 2, Q, H), buf(4, H, Q),
        buf(4, T, E * S), buf(4, T, E * S),
        buf(2, 2, ROWS, H, dtype=F32), buf(2, 2, 2, ROWS, H), buf(2, 2, 2, ROWS, H),
        buf(ROWS, H, dtype=F32), buf(4, ROWS, H), buf(4, ROWS, H),
        buf(2, ROWS, H), buf(2, 2, ROWS, H), buf(4, ROWS, H),
        buf(4, T, Q, dtype=F32), buf(6, T, 128, dtype=F32), buf(4, 1, Q, dtype=F32),
        dma((16,)), dma((2, 4)), dma((2, 4)), dma((2, 4)), dma((2, 4)),
        dma((2, 2)), dma((2, 2)), dma((4,)), dma((4,)),
        dma((4, 2)), dma((4, 2)), dma((4, 2)), dma((4, 2)), dma((4,)), dma((4,)),
        dma((8, 2)), dma((8, 2)), dma((8,)), dma((8,)), dma((8, 2)), dma((8, 2)),
        dma((2, 2)), dma((2, 2)), dma((4,)), dma((4,)), dma((2,)), dma((2,)), dma((4,)), dma((4,)),
        dma((4,)), dma((4,)), dma((8,)), dma((8,)), dma((8,)), dma((8,)), dma((8,)), dma((8,)),
        dma((4,)), dma((4,)), dma((4,)), dma((4,)), dma((2, 4)),
    ]
    out = jax.ShapeDtypeStruct((T, D), BF)
    fwd_out, bwd_out = pl.pallas_call(
        kernel,
        out_shape=(out, out),
        in_specs=[hbm, vmem, hbm, hbm, hbm, vmem, vmem, vmem, hbm, hbm, hbm],
        out_specs=(hbm, hbm),
        scratch_shapes=scratch,
        compiler_params=pltpu.CompilerParams(
            collective_id=0, has_side_effects=True, vmem_limit_bytes=62 * 1024 * 1024
        ),
        cost_estimate=pl.CostEstimate(
            flops=15_000_000_000, bytes_accessed=20_000_000, transcendentals=400_000
        ),
    )(
        fwd_src[0],
        fwd_route.reshape(1, T),
        bwd_input[0],
        bwd_expert_out[0],
        grad_src[0],
        bwd_route.reshape(1, T),
        norm_gain,
        router[0].T,
        gate_w[0].reshape(4, Q, H),
        up_w[0].reshape(4, Q, H),
        down_w[0],
    )
    return (fwd_out[None], bwd_out[None])


def solution(mesh):
    placed = (
        P("pipe", "expert", None),
        P("pipe", "expert", None),
        P("pipe", "expert", None),
        P("pipe", "expert", None),
        P("pipe", "expert", None),
        P("pipe", "expert", None),
        P("pipe", None),
        P("pipe", None, None),
        P("pipe", None, "expert"),
        P("pipe", None, "expert"),
        P("pipe", "expert", None),
    )
    return jax.shard_map(
        shards,
        mesh=mesh,
        in_specs=placed,
        out_specs=(P("pipe", "expert", None), P("pipe", "expert", None)),
        check_vma=False,
    )
```

time: 275 us -> 255 us (0.927)
  Pallas kernels: 264 us -> 249 us
  other arithmetic: 2.99 us -> 0 us
    pallas_call x1, Pallas kernels: 264 us -> 249 us  [shards(): pl.pallas_call(kernel, out_shape=(out, out), in_specs=[hbm, vmem, hbm, hb...]
where the time goes in v2:
time: 255 us; the launch traced here: 254 us
  Pallas kernels  249 us (98%)
  local copies, waits for them, and re-layouts  4.32 us (2%)
    pallas_call x1, Pallas kernels, shards(): pl.pallas_call(kernel, out_shape=(out, out), in_specs=[hbm, vmem, hbm, hb...  249 us

profile of v2, /device:TPU:8, one launch (start us, length us, event | category | flops | bytes accessed | tf_op | source)
XLA Modules:
  0.0 253.9 jit_solution(12477738406140651707)
XLA Ops:
  0.6 249.0 %shard_map.122 = (bf16[64,7168]{1,0:T(8,128)(2,1)}, bf16[64,7168]{1,0:T(8,128)(2,1)}) custom-call(bf16[64,7168]{1,0:T(8,128)(2,1)} %bitcast.19, s32[1,64]{1,0:T(1,128)} %bitcast.24, bf16[64,7168]{1,0:T(8,128)(2,1)} %bitcast.20, bf16[64,7168]{1,0:T(8,128)(2,1)} %bitcast.21, bf16[64,7168]{1,0:T(8,128)(2,1)} %bitcast.22, s32[1,64]{1,0:T(1,128)} %bitcast.25, ...), custom_call_target="tpu_custom_call" | custom-call | flops 15000000512 | bytes 20000000 | tf_op jit(solution)/shard_map/pallas_call | solution.py:517
  249.6 2.2 copy.15
  251.8 2.2 copy.16

commit v3 on v2

--- a/solution.py
+++ b/solution.py
@@ -267,9 +267,6 @@
     for k in (1, 3, 2):
         post(inc.at[(x + k) % 4], xi.at[4 - k], xi_s.at[k], xi_r.at[4 - k], at_x(k))
 
-    for k in (1, 3, 2):
-        post(down_w.at[:, cols((x + k) % 4)], wd.at[4 - k], wd_s.at[k], wd_r.at[4 - k], at_x(k))
-
     for c in load_beo:
         c.wait()
 
@@ -294,6 +291,9 @@
     for c in yb_sends[1]:
         c.wait_send()
     sends += dispatch_half(1, xf, ptf, sbh, rbf, xf_r, yf_s, yf_r)
+
+    for k in (1, 3, 2):
+        post(down_w.at[:, cols((x + k) % 4)], wd.at[4 - k], wd_s.at[k], wd_r.at[4 - k], at_x(k))
 
     fill_i = place(lambda d: xi.at[d], ptb, sbi)
 
@@ -478,6 +478,11 @@
         c.wait_send()
     for c in outs:
         c.wait()
+
+
+def hand_out(fwd_in, bwd_in, fwd_out, bwd_out):
+    fwd_out[...] = fwd_in[...]
+    bwd_out[...] = bwd_in[...]
 
 
 def shards(
@@ -539,6 +544,14 @@
         up_w[0].reshape(4, Q, H),
         down_w[0],
     )
+    rows = pl.BlockSpec((32, D), lambda i: (i, 0))
+    fwd_out, bwd_out = pl.pallas_call(
+        hand_out,
+        out_shape=(out, out),
+        grid=(2,),
+        in_specs=[rows, rows],
+        out_specs=(rows, rows),
+    )(fwd_out, bwd_out)
     return (fwd_out[None], bwd_out[None])
 
 

time: 255 us -> 253 us (level)
  local copies, waits for them, and re-layouts: 4.32 us -> 0 us
    unnamed x2 -> x0, local copies, waits for them, and re-layouts: 4.32 us -> none
where the time goes in v3:
time: 253 us; the launch traced here: 252 us
  Pallas kernels  251 us (99%)
    pallas_call x1, Pallas kernels, shards(): pl.pallas_call(kernel, out_shape=(out, out), in_specs=[hbm, vmem, hbm, hb...  249 us

profile of v3, /device:TPU:8, one launch (start us, length us, event | category | flops | bytes accessed | tf_op | source)
XLA Modules:
  0.0 252.1 jit_solution(10137485498438927144)
XLA Ops:
  0.6 249.0 %shard_map.122 = (bf16[64,7168]{1,0:T(8,128)(2,1)}, bf16[64,7168]{1,0:T(8,128)(2,1)}) custom-call(bf16[64,7168]{1,0:T(8,128)(2,1)} %bitcast.17, s32[1,64]{1,0:T(1,128)} %bitcast.24, bf16[64,7168]{1,0:T(8,128)(2,1)} %bitcast.18, bf16[64,7168]{1,0:T(8,128)(2,1)} %bitcast.19, bf16[64,7168]{1,0:T(8,128)(2,1)} %bitcast.20, s32[1,64]{1,0:T(1,128)} %bitcast.25, ...), custom_call_target="tpu_custom_call" | custom-call | flops 15000000512 | bytes 20000000 | tf_op jit(solution)/shard_map/pallas_call | solution.py:522
  249.6 2.5 shard_map.123

commit v4 on v3

--- a/solution.py
+++ b/solution.py
@@ -179,19 +179,25 @@
         return to_experts(sb.at[j], rb.at[j], lambda o: ys.at[o, j], lambda o: yr.at[o, j])
 
     def gate_up(rb, i):
-        def one(n, _):
+        def others(n, _):
             w, m = n // 2, n % 2
             r = pl.ds(pl.multiple_of(m * 256, 256), 256)
             m4 = pl.ds(m * 4, 4)
-            ra = rb[0, m4].reshape(256, Q)
-            acc[i, w, r, :] = dot(ra, wown[w, 0])
-            ps[i, 0, w, r, :] = dot(ra, wn[0, w]).astype(BF)
-            rc = rb[1, m4].reshape(256, Q)
-            acc[i, w, r, :] += dot(rc, wown[w, 1])
-            ps[i, 1, w, r, :] = dot(rc, wn[1, w]).astype(BF)
+            ps[i, 0, w, r, :] = dot(rb[0, m4].reshape(256, Q), wn[0, w]).astype(BF)
+            ps[i, 1, w, r, :] = dot(rb[1, m4].reshape(256, Q), wn[1, w]).astype(BF)
             return 0
 
-        lax.fori_loop(0, 4, one, 0)
+        def own(n, _):
+            w, m = n // 2, n % 2
+            r = pl.ds(pl.multiple_of(m * 256, 256), 256)
+            m4 = pl.ds(m * 4, 4)
+            acc[i, w, r, :] = dot(rb[0, m4].reshape(256, Q), wown[w, 0])
+            acc[i, w, r, :] += dot(rb[1, m4].reshape(256, Q), wown[w, 1])
+            return 0
+
+        lax.fori_loop(0, 4, others, 0)
+        swap_parts(i)
+        lax.fori_loop(0, 4, own, 0)
 
     def swap_parts(i):
         post(ps.at[i, 0], pr.at[i, 0], rs_s.at[i, 0], rs_r.at[i, 0], at_x(off_a))
@@ -314,12 +320,10 @@
     gate_up(rbb, 0)
 
 
-    swap_parts(0)
     for j in range(2):
         for o in range(8):
             got(rbf.at[j, o], yf_r.at[o, j])
     gate_up(rbf, 1)
-    swap_parts(1)
     for j in range(2):
         got(pr.at[1, j], rs_r.at[1, j])
 

time: 253 us -> 254 us (level)
  no operation moved by 1% of the time
where the time goes in v4:
time: 254 us; the launch traced here: 253 us
  Pallas kernels  253 us (100%)
    pallas_call x1, Pallas kernels, shards(): pl.pallas_call(kernel, out_shape=(out, out), in_specs=[hbm, vmem, hbm, hb...  250 us

profile of v4, /device:TPU:8, one launch (start us, length us, event | category | flops | bytes accessed | tf_op | source)
XLA Modules:
  0.0 253.5 jit_solution(4347283147015929354)
XLA Ops:
  0.6 250.4 %shard_map.122 = (bf16[64,7168]{1,0:T(8,128)(2,1)}, bf16[64,7168]{1,0:T(8,128)(2,1)}) custom-call(bf16[64,7168]{1,0:T(8,128)(2,1)} %bitcast.17, s32[1,64]{1,0:T(1,128)} %bitcast.24, bf16[64,7168]{1,0:T(8,128)(2,1)} %bitcast.18, bf16[64,7168]{1,0:T(8,128)(2,1)} %bitcast.19, bf16[64,7168]{1,0:T(8,128)(2,1)} %bitcast.20, s32[1,64]{1,0:T(1,128)} %bitcast.25, ...), custom_call_target="tpu_custom_call" | custom-call | flops 15000000512 | bytes 20000000 | tf_op jit(solution)/shard_map/pallas_call | solution.py:526
  251.0 2.5 shard_map.123
